TPU v7x, 32 devices: a whole 2x2x4 slice. The times are simulated.
32 devices in a mesh: grp: 4 (over x, core), seq: 4 (over z), tp: 2 (over y).
Axes of the slice: x: 2, y: 2, z: 4, core: 2. Of those that a mesh axis runs over, the one named last changes fastest.
Arguments:
- hidden: bfloat16 [2048, 8192], P(('grp', 'seq')), may hold values from -6 to 6
- queries: bfloat16 [2048, 4096], P(('grp', 'seq'), 'tp'), may hold values from -900 to 900, as said below
- vis_rows: bfloat16 [16, 4, 4, 8192], P(('grp', 'seq')), may hold values from -6 to 6
- vis_slot: int32 [16, 4, 4], P(('grp', 'seq')), may hold values from -1 to 127, as said below
- doc_ids: int32 [4, 512], P('grp', 'seq'), may hold values from 0 to 7, never falling along the last dimension, each value on 1 to 256 neighbouring positions
- w_key: bfloat16 [8192, 512], P('grp', 'tp'), may hold values from -0.0625 to 0.0625
- w_value: bfloat16 [8192, 512], P('grp', 'tp'), may hold values from -0.0625 to 0.0625
Outputs:
- attended: bfloat16 [2048, 4096], P(('grp', 'seq'), 'tp')
Inputs may be any that keep to these rules, and one draw needn't show every extreme that they name: `queries`: a row may be scaled far from one. `vis_slot`: entry [g * 4 + s, d, c] names a position within the 128 positions of index d of seq in group g, or -1. Live positions are distinct within a destination; each device sends 1 to 4 live rows to every destination, slots 0 upward; in every group one destination receives 4 from every device.
All inputs are finite; a program needn't handle non-finite values.
Results may differ from a plain program's by a relative error of at most 0.024.
Values may be sent and summed in bfloat16 or wider, within the bound.
A program may use at most 64 MiB of HBM per device.

v0:
```python
import jax
import jax.numpy as jnp
from jax import lax
from jax.sharding import PartitionSpec as P

HEAD = 128
QPK = 8


def shards(hidden, queries, vis_rows, vis_slot, doc_ids, w_key, w_value):
    tokens = hidden.shape[0]
    width = hidden.shape[1]
    kv_cols = w_key.shape[1]
    kv_local = kv_cols // HEAD
    seq_place = lax.axis_index("seq")
    got_rows, got_slot = (
        lax.all_to_all(vis_rows, "seq", split_axis=1, concat_axis=0, tiled=True),
        lax.all_to_all(vis_slot, "seq", split_axis=1, concat_axis=0, tiled=True),
    )
    extra = got_rows.reshape(-1, width)
    slots = got_slot.reshape(-1)
    piece_key = lax.all_gather(w_key, "grp", axis=0, tiled=True)
    piece_value = lax.all_gather(w_value, "grp", axis=0, tiled=True)
    span = piece_key.shape[0]
    text_keys = jnp.dot(hidden, piece_key, preferred_element_type=jnp.float32)
    text_values = jnp.dot(hidden, piece_value, preferred_element_type=jnp.float32)
    vis_keys = jnp.dot(extra, piece_key, preferred_element_type=jnp.float32)
    vis_values = jnp.dot(extra, piece_value, preferred_element_type=jnp.float32)
    text_keys = text_keys.astype(jnp.bfloat16)
    text_values = text_values.astype(jnp.bfloat16)
    vis_keys = vis_keys.astype(jnp.bfloat16)
    vis_values = vis_values.astype(jnp.bfloat16)
    positions = lax.broadcasted_iota(jnp.int32, (tokens, slots.shape[0]), 0)
    matches = slots[None, :] == positions
    chooser = matches.astype(jnp.bfloat16)
    used = jnp.any(matches, axis=1)[:, None]
    keys = jnp.where(
        used,
        jnp.dot(chooser, vis_keys, preferred_element_type=jnp.float32).astype(jnp.bfloat16),
        text_keys,
    )
    values = jnp.where(
        used,
        jnp.dot(chooser, vis_values, preferred_element_type=jnp.float32).astype(jnp.bfloat16),
        text_values,
    )
    my_docs = doc_ids.reshape(-1)
    query_pos = seq_place * tokens + jnp.arange(tokens, dtype=jnp.int32)
    last_query = seq_place * tokens + tokens - 1
    q_local = queries.reshape(tokens, kv_local, QPK, HEAD)
    scale = 1.0 / jnp.sqrt(jnp.float32(HEAD))
    init_top = jnp.full((kv_local, QPK, tokens), -1e30, jnp.float32)
    init_total = jnp.zeros((kv_local, QPK, tokens), jnp.float32)
    init_acc = jnp.zeros((kv_local, QPK, tokens, HEAD), jnp.float32)
    piece_key = lax.all_gather(keys, "seq", axis=0, tiled=True)
    piece_value = lax.all_gather(values, "seq", axis=0, tiled=True)
    piece_doc = lax.all_gather(my_docs, "seq", axis=0, tiled=True)
    span = piece_key.shape[0]

    def work(state):
        top, total, acc = state
        k_rows = piece_key.reshape(span, kv_local, HEAD)
        v_rows = piece_value.reshape(span, kv_local, HEAD)
        scores = (
            jnp.einsum("tgqd,rgd->gqtr", q_local, k_rows, preferred_element_type=jnp.float32)
            * scale
        )
        key_pos = jnp.arange(span, dtype=jnp.int32)
        allowed = (key_pos[None, :] <= query_pos[:, None]) & (
            piece_doc[None, :] == my_docs[:, None]
        )
        scores = jnp.where(allowed, scores, jnp.float32(-1e30))
        new_top = jnp.maximum(top, jnp.max(scores, axis=-1))
        weights = jnp.where(allowed, jnp.exp(scores - new_top[..., None]), jnp.float32(0.0))
        total = jnp.sum(weights, axis=-1)
        acc = jnp.einsum(
            "gqtr,rgd->gqtd",
            weights.astype(jnp.bfloat16),
            v_rows,
            preferred_element_type=jnp.float32,
        )
        return (new_top, total, acc)

    top, total, acc = lax.cond(
        jnp.int32(0) > last_query, lambda state: state, work, (init_top, init_total, init_acc)
    )
    result = acc / total[..., None]
    return result.transpose(2, 0, 1, 3).reshape(tokens, kv_local * QPK * HEAD).astype(jnp.bfloat16)


def solution(mesh):
    return jax.shard_map(
        shards,
        mesh=mesh,
        in_specs=(
            P(("grp", "seq"), None),
            P(("grp", "seq"), "tp"),
            P(("grp", "seq"), None, None, None),
            P(("grp", "seq"), None, None),
            P("grp", "seq"),
            P("grp", "tp"),
            P("grp", "tp"),
        ),
        out_specs=P(("grp", "seq"), "tp"),
        check_vma=False,
    )
```

profile of v0, /device:TPU:0, one launch (start us, length us, event | category | flops | bytes accessed | tf_op | source)
XLA Modules:
  0.0 120.2 jit_solution(4710813715158930798)
XLA Ops:
  6.5 0.0 copy-start
  6.5 0.0 all-gather.6.cloned.1.call-start
  6.5 0.7 all-gather.6.cloned.1.call-update
  7.3 0.0 all-gather.4.cloned.1.call-start
  7.3 0.7 all-gather.4.cloned.1.call-update
  8.0 11.8 %all_to_all.8 = s32[1,4,4]{2,0,1:T(1,128)S(1)} all-to-all(s32[1,4,4]{2,0,1:T(1,128)} %bitcast.45), channel_id=1, replica_groups=mesh['grp'=4,'seq'=4,'tp'=2] {'seq'}, dimensions={1} | all-to-all | bytes 128 | tf_op jit(solution)/shard_map/all_to_all | solution.py:18
  19.8 3.4 %all-to-all-start.1 = ((bf16[1,4,4,8192]{3,2,0,1:T(4,128)(2,1)}), bf16[1,4,4,8192]{3,2,0,1:T(4,128)(2,1)S(1)}, u32[]{:S(2)}, u32[]{:S(2)}) async-start(bf16[1,4,4,8192]{3,2,0,1:T(4,128)(2,1)} %bitcast.41), calls=%async_computation.1 | async-start | bytes 524288 | tf_op jit(solution)/shard_map/all_to_all | solution.py:17
  23.2 11.4 %all-gather = s32[1,512]{1,0:T(1,128)S(1)} all-gather(s32[1,128]{1,0:T(1,128)} %param.13), channel_id=2, replica_groups=mesh['grp'=4,'seq'=4,'tp'=2] {'seq'}, dimensions={1}, use_global_device_ids=true | all-gather | bytes 2560 | tf_op jit(solution)/shard_map/all_gather | solution.py:57
  34.7 0.5 broadcast.20
  35.2 0.7 reduce.3
  35.8 0.1 eq.25
  35.9 0.1 fusion.17
  36.0 0.0 all-to-all-done.1
  36.0 0.1 reshape.36
  36.1 10.0 %all-gather.6.cloned.1.call-done = bf16[8192,256]{1,0:T(8,128)(2,1)} async-done(((bf16[2048,256]{1,0:T(8,128)(2,1)}), bf16[8192,256]{1,0:T(8,128)(2,1)}) %all-gather.6.cloned.1.call-update) | async-done | bytes 4194320 | tf_op jit(solution)/shard_map/all_gather | solution.py:23
  46.1 0.0 copy-done
  46.1 2.9 %convolution_convert_fusion = bf16[128,256]{1,0:T(8,128)(2,1)S(1)} fusion(bf16[128,8192]{1,0:T(8,128)(2,1)S(1)} %copy-done, bf16[8192,256]{1,0:T(8,128)(2,1)} %all-gather.6.cloned.1.call-done), kind=kOutput, calls=%fused_computation.18 | convolution fusion | flops 536903680 | bytes 6356992 | tf_op jit(solution)/shard_map/dot_general | solution.py:26
  49.0 3.0 %fusion.15 = bf16[128,256]{1,0:T(8,128)(2,1)S(1)} fusion(bf16[128,256]{1,0:T(8,128)(2,1)S(1)} %convolution_convert_fusion, bf16[16,8192]{1,0:T(8,128)(2,1)S(1)} %reshape.36, bf16[8192,256]{1,0:T(8,128)(2,1)} %all-gather.6.cloned.1.call-done, pred[128]{0:T(512)(128)(4,1)S(1)} %fusion.17, s32[16]{0:T(128)S(1)} %eq.25), kind=kOutput, calls=%fused_computation.23 | convolution fusion | flops 68229120 | bytes 4587712 | tf_op jit(solution)/shard_map/dot_general | solution.py:44
  52.1 13.9 %all_gather.19 = bf16[512,256]{1,0:T(8,128)(2,1)S(1)} all-gather(bf16[128,256]{1,0:T(8,128)(2,1)S(1)} %fusion.15), channel_id=1, replica_groups=mesh['grp'=4,'seq'=4,'tp'=2] {'seq'}, dimensions={0}, use_global_device_ids=true | all-gather | bytes 327680 | tf_op jit(solution)/shard_map/all_gather | solution.py:56
  65.9 0.0 copy-start.2
  65.9 16.3 %all-gather.4.cloned.1.call-done = bf16[8192,256]{1,0:T(8,128)(2,1)} async-done(((bf16[2048,256]{1,0:T(8,128)(2,1)}), bf16[8192,256]{1,0:T(8,128)(2,1)}) %all-gather.4.cloned.1.call-update) | async-done | bytes 4194320 | tf_op jit(solution)/shard_map/all_gather | solution.py:22
  82.2 2.9 %convolution_convert_fusion.2 = bf16[128,256]{1,0:T(8,128)(2,1)S(1)} fusion(bf16[128,8192]{1,0:T(8,128)(2,1)S(1)} %copy-done, bf16[8192,256]{1,0:T(8,128)(2,1)} %all-gather.4.cloned.1.call-done), kind=kOutput, calls=%fused_computation.20 | convolution fusion | flops 536903680 | bytes 6356992 | tf_op jit(solution)/shard_map/dot_general | solution.py:25
  85.1 3.0 %fusion.14 = bf16[128,256]{1,0:T(8,128)(2,1)S(1)} fusion(bf16[128,256]{1,0:T(8,128)(2,1)S(1)} %convolution_convert_fusion.2, bf16[16,8192]{1,0:T(8,128)(2,1)S(1)} %reshape.36, bf16[8192,256]{1,0:T(8,128)(2,1)} %all-gather.4.cloned.1.call-done, pred[128]{0:T(512)(128)(4,1)S(1)} %fusion.17, s32[16]{0:T(128)S(1)} %eq.25), kind=kOutput, calls=%fused_computation.22 | convolution fusion | flops 68229120 | bytes 4587712 | tf_op jit(solution)/shard_map/dot_general | solution.py:39
  88.1 13.9 %all_gather.17 = bf16[512,256]{1,0:T(8,128)(2,1)S(1)} all-gather(bf16[128,256]{1,0:T(8,128)(2,1)S(1)} %fusion.14), channel_id=1, replica_groups=mesh['grp'=4,'seq'=4,'tp'=2] {'seq'}, dimensions={0}, use_global_device_ids=true | all-gather | bytes 327680 | tf_op jit(solution)/shard_map/all_gather | solution.py:55
  102.1 0.0 copy-done.2
  102.1 9.7 %conditional.1 = (f32[2,8,128]{2,1,0:T(8,128)S(1)}, f32[2,8,128,128]{3,2,1,0:T(8,128)S(1)}) conditional(s32[]{:T(128)} %convert_element_type.34, (s32[]{:T(128)}, s32[128]{0:T(128)S(1)}, s32[512]{0:T(512)S(1)}, s32[1,128]{1,0:T(1,128)S(1)}, bf16[512,256]{1,0:T(8,128)(2,1)S(1)}, /*index=5*/bf16[128,2048]{1,0:T(8,128)(2,1)}, ...), branch_computations={%region_1.4_spmd, %region_4.5_spmd} | conditional | flops 550697088 | bytes 33869872 | solution.py:84
  102.1 0.1 fusion.10
  102.2 1.1 copy.42
  103.4 0.1 reshape.30
  103.5 2.7 %fusion = (f32[2,8,128]{2,1,0:T(8,128)S(1)}, f32[2,512,128,8]{2,1,3,0:T(8,128)}) fusion(pred[128,512]{0,1:T(8,128)(4,1)S(1)} %fusion.10, bf16[128,2,8,128]{3,2,1,0:T(8,128)(2,1)S(1)} %bitcast.38, bf16[512,2,128,1]{2,1,0,3:T(2,128)(2,1)S(1)} %bitcast.40), kind=kOutput, calls=%fused_computation.2 | convolution fusion | flops 271579136 | bytes 5054464 | tf_op jit(solution)/shard_map/cond/branch_0_fun/tgqd,rgd->gqtr/dot_general | solution.py:65
  106.2 0.8 reshape.32
  107.0 0.0 copy-start.1
  107.0 3.7 %fusion.3 = f32[2,8,128,128]{3,2,1,0:T(8,128)S(1)} fusion(f32[2,512,128,8]{2,1,3,0:T(8,128)} %get-tuple-element.36, f32[2,8,128]{2,1,0:T(8,128)S(1)} %broadcast_maximum_fusion, pred[128,512]{0,1:T(8,128)(4,1)S(1)} %fusion.10, bf16[512,2,128,1]{2,1,0,3:T(2,128)(2,1)} %bitcast.42), kind=kOutput, calls=%fused_computation.5 | convolution fusion | flops 273678336 | bytes 5578752 | tf_op jit(solution)/shard_map/cond/branch_0_fun/gqtr,rgd->gqtd/dot_general | solution.py:76
  110.7 0.0 copy-done.1
  110.7 1.0 fusion.2
  111.8 0.3 fusion.16
  112.1 0.3 copy.34
  112.5 0.9 copy.55
  (3 shorter events, 0.0 us)
Async XLA Ops:
  6.5 39.6 %copy-start = (bf16[128,8192]{1,0:T(8,128)(2,1)S(1)}, bf16[128,8192]{1,0:T(8,128)(2,1)}, u32[]{:S(2)}) copy-start(bf16[128,8192]{1,0:T(8,128)(2,1)} %param.9) | copy-start | bytes 6291460
  6.5 39.6 %all-gather.6.cloned.1.call-start = ((), (), s32[]{:S(2)}) async-start(), calls=%async_computation.3 | async-start | bytes 5242880 | tf_op jit(solution)/shard_map/all_gather | solution.py:23
  7.3 74.9 %all-gather.4.cloned.1.call-start = ((), (), s32[]{:S(2)}) async-start(), calls=%async_computation.2 | async-start | bytes 5242880 | tf_op jit(solution)/shard_map/all_gather | solution.py:22
  19.8 16.2 %all-to-all-start.1 = ((bf16[1,4,4,8192]{3,2,0,1:T(4,128)(2,1)}), bf16[1,4,4,8192]{3,2,0,1:T(4,128)(2,1)S(1)}, u32[]{:S(2)}, u32[]{:S(2)}) async-start(bf16[1,4,4,8192]{3,2,0,1:T(4,128)(2,1)} %bitcast.41), calls=%async_computation.1 | async-start | bytes 524288 | tf_op jit(solution)/shard_map/all_to_all | solution.py:17
  65.9 36.2 %copy-start.2 = (s32[1,128]{1,0:T(1,128)S(1)}, s32[1,128]{1,0:T(1,128)}, u32[]{:S(2)}) copy-start(s32[1,128]{1,0:T(1,128)} %param.13) | copy-start | bytes 1540
  107.0 3.8 %copy-start.1 = (f32[2,512,128,8]{2,1,3,0:T(8,128)S(1)}, f32[2,512,128,8]{2,1,3,0:T(8,128)}, u32[]{:S(2)}) copy-start(f32[2,512,128,8]{2,1,3,0:T(8,128)} %get-tuple-element.36) | copy-start | bytes 12582916 | tf_op jit(solution)/shard_map/cond
Sparse Core Ops, SparseCore 0:
  8.9 37.1 all-gather.5
  47.7 34.4 all-gather.3
where the time goes:
time: 121 us; the launch traced here: 120 us
  blocking collectives  51 us (42%)
  waiting for transfers between devices  27.7 us (23%)
  matrix products  18.3 us (15%)
  between operations  13.5 us (11%)
  local copies, waits for them, and re-layouts  3.93 us (3%)
  starting transfers between devices  3.45 us (3%)
  other arithmetic  2.27 us (2%)
    all_gather x1, waiting for transfers between devices, shards(): piece_key = lax.all_gather(w_key, 'grp', axis=0, tiled=True)  16.3 us
    all_gather x1, blocking collectives, shards(): piece_key = lax.all_gather(keys, 'seq', axis=0, tiled=True)  13.9 us
    all_gather x1, blocking collectives, shards(): piece_value = lax.all_gather(values, 'seq', axis=0, tiled=True)  13.9 us
    all_to_all x1, blocking collectives, shards(): lax.all_to_all(vis_slot, 'seq', split_axis=1, concat_axis=0, tiled=True)  11.8 us
    all_gather x1, blocking collectives, shards(): piece_doc = lax.all_gather(my_docs, 'seq', axis=0, tiled=True)  11.4 us
    all_gather x1, waiting for transfers between devices, shards(): piece_value = lax.all_gather(w_value, 'grp', axis=0, tiled=True)  10 us
    dot_general x1, matrix products, work(): jnp.einsum('gqtr,rgd->gqtd', weights.astype(jnp.bfloat16), v_rows, prefer...  3.75 us
    all_to_all x1, starting transfers between devices, shards(): lax.all_to_all(vis_rows, 'seq', split_axis=1, concat_axis=0, tiled=True)  3.41 us
  transfers between devices with their start and end apart: 3, of which 2 were waited for; matrix products, arithmetic and copies ran while one was open for 6% of the time, Pallas kernels for 0%

commit v1 on v0

v1 whole, which is shorter than its diff:
```python
import functools

import jax
import jax.numpy as jnp
from jax import lax
from jax.experimental import pallas as pl
from jax.experimental.pallas import tpu as pltpu
from jax.sharding import PartitionSpec as P

HEAD = 128
QPK = 8
F32 = jnp.float32
BF16 = jnp.bfloat16
MESH = pl.DeviceIdType.MESH


def kernel(
    G, S, T,
    hid, vis, qry, wk, wv, pos, docs, out,
    w, hown, hb, part, back, total, kvt, kvv, posb, docb, qs, top, den, acc,
    loc, hs, hr, rs, rr, bs, br, ts, tr, vs, vr, ms, mr,
):
    tok, V = hid.shape[0], vis.shape[0]
    dw, kvc = wk.shape
    nkv = kvc // HEAD
    C = dw // T
    rows = tok + V
    half = tok // 2
    g, s, t = lax.axis_index("grp"), lax.axis_index("seq"), lax.axis_index("tp")
    X = G // 2
    offs = [(ox, oc) for ox in range(X) for oc in range(2) if ox or oc]
    far = [i for i, o in enumerate(offs) if o[0]]
    chunks = [(0, half), (half, rows - half)]

    def to_grp(o, sign):
        ox, oc = o
        return lax.rem(g // 2 + (X + sign * ox), X) * 2 + lax.rem(g % 2 + oc, 2)

    def peer_tp(dt):
        return lax.rem(t + dt, T)

    loads = [
        pltpu.make_async_copy(wk, w.at[:, pl.ds(0, kvc)], loc.at[0]),
        pltpu.make_async_copy(wv, w.at[:, pl.ds(kvc, kvc)], loc.at[1]),
        pltpu.make_async_copy(
            hid.at[:, pl.ds(pl.multiple_of(g * dw, 128), dw)], hown.at[pl.ds(0, tok)], loc.at[2]
        ),
        pltpu.make_async_copy(
            vis.at[:, pl.ds(pl.multiple_of(g * dw, 128), dw)], hown.at[pl.ds(tok, V)], loc.at[3]
        ),
    ]
    qloads = [
        pltpu.make_async_copy(
            qry.at[:, pl.ds((k * QPK + h) * HEAD, HEAD)],
            qs.at[k, pl.ds(h * tok, tok)],
            loc.at[4 + k * QPK + h],
        )
        for k in range(nkv)
        for h in range(QPK)
    ]

    barrier = pltpu.get_barrier_semaphore()
    for o in offs:
        pl.semaphore_signal(barrier, inc=1, device_id={"grp": to_grp(o, 1)}, device_id_type=MESH)
    for d in range(1, S):
        pl.semaphore_signal(
            barrier, inc=1, device_id={"seq": lax.rem(s + d, S)}, device_id_type=MESH
        )
    for d in range(1, T):
        pl.semaphore_signal(barrier, inc=1, device_id={"tp": peer_tp(d)}, device_id_type=MESH)
    for c in loads:
        c.start()
    pl.semaphore_wait(barrier, (G - 1) + (S - 1) + (T - 1))

    def piece(i, ch):
        o = offs[i]
        whom = to_grp(o, 1)
        start = 0 if i not in far else t * C
        wide = dw if i not in far else C
        src_col = pl.multiple_of(whom * dw + start, 128)
        dst_col = pl.multiple_of(start, 128) if i in far else 0
        lo = ch * half
        made = [
            pltpu.make_async_remote_copy(
                src_ref=hid.at[pl.ds(lo, half), pl.ds(src_col, wide)],
                dst_ref=hb.at[i, pl.ds(lo, half), pl.ds(dst_col, wide)],
                send_sem=hs.at[i, ch],
                recv_sem=hr.at[i, ch],
                device_id={"grp": whom},
                device_id_type=MESH,
            )
        ]
        if ch == 1:
            made.append(
                pltpu.make_async_remote_copy(
                    src_ref=vis.at[:, pl.ds(src_col, wide)],
                    dst_ref=hb.at[i, pl.ds(tok, V), pl.ds(dst_col, wide)],
                    send_sem=hs.at[i, 2],
                    recv_sem=hr.at[i, 2],
                    device_id={"grp": whom},
                    device_id_type=MESH,
                )
            )
        return made

    pieces = {(i, ch): piece(i, ch) for i in range(len(offs)) for ch in range(2)}
    items = [(i, ch) for ch in range(2) for i in far]
    near = [i for i in range(len(offs)) if i not in far]
    for it in items + [(i, ch) for i in near for ch in range(2)]:
        for c in pieces[it]:
            c.start()

    posb[pl.ds(pl.multiple_of(s * V, V), V), :] = pos[...]
    docb[s] = docs[...]
    metas = []
    for d in range(1, S):
        whom = lax.rem(s + d, S)
        metas.append(
            pltpu.make_async_remote_copy(
                src_ref=pos, dst_ref=posb.at[pl.ds(pl.multiple_of(s * V, V), V)],
                send_sem=ms.at[d, 0], recv_sem=mr.at[d, 0],
                device_id={"seq": whom}, device_id_type=MESH,
            )
        )
        metas.append(
            pltpu.make_async_remote_copy(
                src_ref=docs, dst_ref=docb.at[s],
                send_sem=ms.at[d, 1], recv_sem=mr.at[d, 1],
                device_id={"seq": whom}, device_id_type=MESH,
            )
        )
    for c in metas:
        c.start()
    for c in qloads:
        c.start()

    for c in loads:
        c.wait()
    total[...] = jnp.dot(hown[...], w[...], preferred_element_type=F32)

    def relay(i, ch):
        lo, n = chunks[ch]
        at = hb.at[i, pl.ds(lo, n), pl.ds(pl.multiple_of(t * C, 128), C)]
        return [
            pltpu.make_async_remote_copy(
                src_ref=at, dst_ref=at,
                send_sem=rs.at[i, ch, d], recv_sem=rr.at[i, ch, d],
                device_id={"tp": peer_tp(d)}, device_id_type=MESH,
            )
            for d in range(1, T)
        ]

    relays = {it: relay(*it) for it in items}

    def giveback(i, ch):
        lo, n = chunks[ch]
        return pltpu.make_async_remote_copy(
            src_ref=part.at[i, pl.ds(lo, n)], dst_ref=back.at[i, pl.ds(lo, n)],
            send_sem=bs.at[i, ch], recv_sem=br.at[i, ch],
            device_id={"grp": to_grp(offs[i], -1)}, device_id_type=MESH,
        )

    gives = {(i, ch): giveback(i, ch) for i in range(len(offs)) for ch in range(2)}

    def project(i, ch):
        lo, n = chunks[ch]
        part[i, lo:lo + n, :] = jnp.dot(
            hb[i, lo:lo + n, :], w[...], preferred_element_type=F32
        ).astype(BF16)
        gives[i, ch].start()

    def finish(it):
        for c in relays[it]:
            c.wait_recv()
        project(*it)

    for at, it in enumerate(items):
        for c in pieces[it]:
            c.wait_recv()
        for c in relays[it]:
            c.start()
        if at == 0:
            for i in near:
                for ch in range(2):
                    for c in pieces[i, ch]:
                        c.wait_recv()
                    project(i, ch)
        else:
            finish(items[at - 1])
    finish(items[-1])

    def text(d, ch):
        here = kvt.at[s, pl.ds(ch * half, half)]
        return pltpu.make_async_remote_copy(
            src_ref=here, dst_ref=here,
            send_sem=ts.at[d, ch], recv_sem=tr.at[s, ch],
            device_id={"seq": d}, device_id_type=MESH,
        )

    vrow = pl.ds(pl.multiple_of(s * V, V), V)

    def visual(d):
        whom = lax.rem(s + d, S)
        return pltpu.make_async_remote_copy(
            src_ref=kvv.at[vrow], dst_ref=kvv.at[vrow],
            send_sem=vs.at[d], recv_sem=vr.at[d],
            device_id={"seq": whom}, device_id_type=MESH,
        )

    visuals = [visual(d) for d in range(1, S)]
    for ch in range(2):
        lo, n = chunks[ch]
        both = total[lo:lo + n, :]
        for i in range(len(offs)):
            gives[i, ch].wait_recv()
            both = both + back[i, lo:lo + n, :].astype(F32)
        both = both.astype(BF16)
        kvt[s, lo:lo + half, :] = both[:half]
        if ch == 1:
            kvv[vrow, :] = both[half:]
            for c in visuals:
                c.start()
        for d in range(S - 1, 0, -1):
            @pl.when(d > s)
            def _():
                text(d, ch).start()

    for c in qloads:
        c.wait()
    for c in metas:
        c.wait_recv()
    for c in visuals:
        c.wait_recv()
    scale = 1.0 / (HEAD ** 0.5)
    lanes = lax.broadcasted_iota(jnp.int32, (S * V, tok), 1)
    krow = lax.broadcasted_iota(jnp.int32, (tok, tok), 0)
    qcol = lax.broadcasted_iota(jnp.int32, (tok, tok), 1)
    qdoc = jnp.broadcast_to(docs[...].astype(F32), (tok, tok))
    top[...] = jnp.full(top.shape, -1e30, F32)
    den[...] = jnp.zeros(den.shape, F32)
    acc[...] = jnp.zeros(acc.shape, F32)
    firsts = (((0,), (0,)), ((), ()))

    def block(j):
        pick = (posb[...] == lanes + j * tok).astype(F32).astype(BF16)
        moved = lax.dot_general(pick, kvv[...], firsts, preferred_element_type=F32)
        used = lax.dot_general(
            pick, jnp.ones((S * V, 2 * kvc), BF16), firsts, preferred_element_type=F32
        )
        kv = jnp.where(used > 0.5, moved, kvt[j].astype(F32)).astype(BF16)
        kdoc = jnp.broadcast_to(docb[j].astype(F32), (tok, tok)).T
        allowed = (krow + j * tok <= qcol + s * tok) & (kdoc == qdoc)
        bias = jnp.where(allowed, F32(0.0), F32(-1e30))
        bias = jnp.concatenate([bias] * QPK, axis=1)
        for k in range(nkv):
            key = kv[:, k * HEAD:(k + 1) * HEAD]
            value = kv[:, kvc + k * HEAD:kvc + (k + 1) * HEAD]
            scores = lax.dot_general(
                key, qs[k], (((1,), (1,)), ((), ())), preferred_element_type=F32
            ) * scale + bias
            old = top[k]
            new = jnp.maximum(old, jnp.max(scores, axis=0, keepdims=True))
            weights = jnp.exp(scores - new)
            shrink = jnp.exp(old - new)
            top[k] = new
            den[k] = den[k] * shrink + jnp.sum(weights, axis=0, keepdims=True)
            acc[k] = acc[k] * shrink + lax.dot_general(
                value, weights.astype(BF16), firsts, preferred_element_type=F32
            )

    block(s)

    def step(i, carry):
        j = s - i
        for ch in range(2):
            there = kvt.at[j, pl.ds(ch * half, half)]
            pltpu.make_async_remote_copy(
                src_ref=there, dst_ref=there,
                send_sem=ts.at[0, ch], recv_sem=tr.at[j, ch],
                device_id={"seq": j}, device_id_type=MESH,
            ).wait_recv()
        block(j)
        return carry

    lax.fori_loop(1, s + 1, step, 0)
    for k in range(nkv):
        done = acc[k] / den[k]
        for h in range(QPK):
            at = (k * QPK + h) * HEAD
            out[:, at:at + HEAD] = done[:, h * tok:(h + 1) * tok].T.astype(out.dtype)

    for it in pieces.values():
        for c in it:
            c.wait_send()
    for it in relays.values():
        for c in it:
            c.wait_send()
    for c in gives.values():
        c.wait_send()
    for c in metas + visuals:
        c.wait_send()
    for ch in range(2):
        for d in range(1, S):
            @pl.when(d > s)
            def _():
                text(d, ch).wait_send()


def shards(G, S, T, hidden, queries, vis_rows, vis_slot, doc_ids, w_key, w_value):
    tok, D = hidden.shape
    vis = vis_rows.reshape(-1, D)
    V = vis.shape[0]
    dw, kvc = w_key.shape
    nkv = kvc // HEAD
    slot = vis_slot.reshape(S, -1)
    place = jnp.arange(S, dtype=jnp.int32)[:, None] * tok + slot
    pos = jnp.where(slot >= 0, place, -1).reshape(V, 1)
    pos = jnp.broadcast_to(pos, (V, tok)).astype(jnp.int32)
    rows = tok + V
    dma = pltpu.SemaphoreType.DMA
    hbm = pl.BlockSpec(memory_space=pl.ANY)
    vmem = pl.BlockSpec(memory_space=pltpu.VMEM)
    return pl.pallas_call(
        functools.partial(kernel, G, S, T),
        out_shape=jax.ShapeDtypeStruct((tok, queries.shape[1]), BF16),
        in_specs=[hbm, hbm, hbm, hbm, hbm, vmem, vmem],
        out_specs=vmem,
        scratch_shapes=[
            pltpu.VMEM((dw, 2 * kvc), BF16),
            pltpu.VMEM((rows, dw), BF16),
            pltpu.VMEM((G - 1, rows, dw), BF16),
            pltpu.VMEM((G - 1, rows, 2 * kvc), BF16),
            pltpu.VMEM((G - 1, rows, 2 * kvc), BF16),
            pltpu.VMEM((rows, 2 * kvc), F32),
            pltpu.VMEM((S, tok, 2 * kvc), BF16),
            pltpu.VMEM((S * V, 2 * kvc), BF16),
            pltpu.VMEM((S * V, tok), jnp.int32),
            pltpu.VMEM((S, 1, tok), jnp.int32),
            pltpu.VMEM((nkv, QPK * tok, HEAD), BF16),
            pltpu.VMEM((nkv, 1, QPK * tok), F32),
            pltpu.VMEM((nkv, 1, QPK * tok), F32),
            pltpu.VMEM((nkv, HEAD, QPK * tok), F32),
            dma((4 + nkv * QPK,)),
            dma((G - 1, 3)), dma((G - 1, 3)),
            dma((G - 1, 2, T)), dma((G - 1, 2, T)),
            dma((G - 1, 2)), dma((G - 1, 2)),
            dma((S, 2)), dma((S, 2)),
            dma((S,)), dma((S,)),
            dma((S, 2)), dma((S, 2)),
        ],
        compiler_params=pltpu.CompilerParams(
            collective_id=0, has_side_effects=True, vmem_limit_bytes=40 * 1024 * 1024
        ),
    )(hidden, vis, queries, w_key, w_value, pos, doc_ids)


def solution(mesh):
    sizes = mesh.shape
    return jax.shard_map(
        functools.partial(shards, sizes["grp"], sizes["seq"], sizes["tp"]),
        mesh=mesh,
        in_specs=(
            P(("grp", "seq"), None),
            P(("grp", "seq"), "tp"),
            P(("grp", "seq"), None, None, None),
            P(("grp", "seq"), None, None),
            P("grp", "seq"),
            P("grp", "tp"),
            P("grp", "tp"),
        ),
        out_specs=P(("grp", "seq"), "tp"),
        check_vma=False,
    )
```

time: 121 us -> 49.2 us (0.41)
  the two profiles are of different devices: /device:TPU:0 before, /device:TPU:17 now
where the time goes in v1:
time: 49.2 us; the launch traced here: 48.9 us
  Pallas kernels  40.3 us (82%)
  local copies, waits for them, and re-layouts  8.54 us (17%)
    pallas_call x1, Pallas kernels, shards(): pl.pallas_call(functools.partial(kernel, G, S, T), out_shape=jax.ShapeDty...  40.3 us
    unnamed x11, local copies, waits for them, and re-layouts  6.53 us
    reshape x1, local copies, waits for them, and re-layouts, shards(): vis = vis_rows.reshape(-1, D)  1.02 us

profile of v1, /device:TPU:17, one launch (start us, length us, event | category | flops | bytes accessed | tf_op | source)
XLA Modules:
  0.0 48.9 jit_solution(13665213200146156794)
XLA Ops:
  0.0 0.8 %reshape.29 = s32[16]{0:T(128)S(1)} reshape(s32[1,4,4]{2,1,0:T(4,128)} %param.10) | data formatting | bytes 128 | tf_op jit(solution)/shard_map/reshape | solution.py:315
  0.8 0.1 add.14
  0.8 0.1 add.15
  0.9 0.1 broadcast_in_dim.11.pos
  1.0 1.0 %reshape.28.vis = bf16[16,8192]{1,0:T(8,128)(2,1)S(1)} reshape(bf16[1,4,4,8192]{3,2,1,0:T(4,128)(2,1)} %param.9) | data formatting | bytes 524288 | tf_op jit(solution)/shard_map/reshape | solution.py:311
  2.0 0.0 copy-start
  2.0 1.6 %copy-done = bf16[128,8192]{1,0:T(8,128)(2,1)S(1)} copy-done((bf16[128,8192]{1,0:T(8,128)(2,1)S(1)}, bf16[128,8192]{1,0:T(8,128)(2,1)}, u32[]{:S(2)}) %copy-start) | copy-done | bytes 2097176
  3.6 0.0 copy-start.1
  3.6 1.2 %copy-done.1 = bf16[2048,256]{1,0:T(8,128)(2,1)S(1)} copy-done((bf16[2048,256]{1,0:T(8,128)(2,1)S(1)}, bf16[2048,256]{1,0:T(8,128)(2,1)}, u32[]{:S(2)}) %copy-start.1) | copy-done | bytes 1048600
  4.8 0.0 copy-start.2
  4.9 1.2 %copy-done.2 = bf16[2048,256]{1,0:T(8,128)(2,1)S(1)} copy-done((bf16[2048,256]{1,0:T(8,128)(2,1)S(1)}, bf16[2048,256]{1,0:T(8,128)(2,1)}, u32[]{:S(2)}) %copy-start.2) | copy-done | bytes 1048600
  6.1 0.0 copy-start.3
  6.1 1.0 %copy-done.3 = bf16[128,2048]{1,0:T(8,128)(2,1)S(1)} copy-done((bf16[128,2048]{1,0:T(8,128)(2,1)S(1)}, bf16[128,2048]{1,0:T(8,128)(2,1)}, u32[]{:S(2)}) %copy-start.3) | copy-done | bytes 524312
  7.1 0.0 copy-start.4
  7.1 0.7 %copy-done.4 = s32[1,128]{1,0:T(1,128)S(1)} copy-done((s32[1,128]{1,0:T(1,128)S(1)}, s32[1,128]{1,0:T(1,128)}, u32[]{:S(2)}) %copy-start.4) | copy-done | bytes 536
  7.8 40.3 %shard_map.73 = bf16[128,2048]{1,0:T(8,128)(2,1)S(1)} custom-call(bf16[128,8192]{1,0:T(8,128)(2,1)S(1)} %copy-done, bf16[16,8192]{1,0:T(8,128)(2,1)S(1)} %reshape.28.vis, bf16[128,2048]{1,0:T(8,128)(2,1)S(1)} %copy-done.3, bf16[2048,256]{1,0:T(8,128)(2,1)S(1)} %copy-done.1, bf16[2048,256]{1,0:T(8,128)(2,1)S(1)} %copy-done.2, ...), custom_call_target="tpu_custom_call" | custom-call | tf_op jit(solution)/shard_map/pallas_call | solution.py:323
  48.1 0.8 %copy.9 = bf16[128,2048]{1,0:T(8,128)(2,1)} copy(bf16[128,2048]{1,0:T(8,128)(2,1)S(1)} %shard_map.73) | data formatting | bytes 1048576
  (2 shorter events, 0.0 us)
Async XLA Ops:
  2.0 1.6 %copy-start = (bf16[128,8192]{1,0:T(8,128)(2,1)S(1)}, bf16[128,8192]{1,0:T(8,128)(2,1)}, u32[]{:S(2)}) copy-start(bf16[128,8192]{1,0:T(8,128)(2,1)} %hid.1) | copy-start | bytes 6291460
  3.6 1.2 %copy-start.1 = (bf16[2048,256]{1,0:T(8,128)(2,1)S(1)}, bf16[2048,256]{1,0:T(8,128)(2,1)}, u32[]{:S(2)}) copy-start(bf16[2048,256]{1,0:T(8,128)(2,1)} %wk.1) | copy-start | bytes 3145732
  4.8 1.2 %copy-start.2 = (bf16[2048,256]{1,0:T(8,128)(2,1)S(1)}, bf16[2048,256]{1,0:T(8,128)(2,1)}, u32[]{:S(2)}) copy-start(bf16[2048,256]{1,0:T(8,128)(2,1)} %wv.1) | copy-start | bytes 3145732
  6.1 1.0 %copy-start.3 = (bf16[128,2048]{1,0:T(8,128)(2,1)S(1)}, bf16[128,2048]{1,0:T(8,128)(2,1)}, u32[]{:S(2)}) copy-start(bf16[128,2048]{1,0:T(8,128)(2,1)} %qry.1) | copy-start | bytes 1572868
  7.1 0.7 %copy-start.4 = (s32[1,128]{1,0:T(1,128)S(1)}, s32[1,128]{1,0:T(1,128)}, u32[]{:S(2)}) copy-start(s32[1,128]{1,0:T(1,128)} %docs.1) | copy-start | bytes 1540

commit v2 on v1

v2 whole, which is shorter than its diff:
```python
import functools

import jax
import jax.numpy as jnp
from jax import lax
from jax.experimental import pallas as pl
from jax.experimental.pallas import tpu as pltpu
from jax.sharding import PartitionSpec as P

HEAD = 128
QPK = 8
F32 = jnp.float32
BF16 = jnp.bfloat16
MESH = pl.DeviceIdType.MESH


def kernel(
    G, S, T, Q,
    hid, visin, qry, wk, wv, slots, docin, out,
    w, hown, hb, part, back, total, kvt, kvv, posb, docb, qs, top, den, acc,
    visl, vis, slotl, pos, docs,
    loc, hs, hr, rs, rr, bs, br, ts, tr, vs, vr, ms, mr,
):
    tok, V = hid.shape[0], vis.shape[0]
    dw, kvc = wk.shape
    nkv = kvc // HEAD
    cap = V // S
    C = dw // T
    rows = tok + V
    q = tok // Q
    g, s, t = lax.axis_index("grp"), lax.axis_index("seq"), lax.axis_index("tp")
    X = G // 2
    offs = [(ox, oc) for ox in range(X) for oc in range(2) if ox or oc]
    far = [i for i, o in enumerate(offs) if o[0]]
    near = [i for i, o in enumerate(offs) if not o[0]]
    chunks = [(0, V + q)] + [(V + c * q, q) for c in range(1, Q)]
    mine = pl.ds(pl.multiple_of(g * dw, 128), dw)

    def to_grp(o, sign):
        ox, oc = o
        return lax.rem(g // 2 + (X + sign * ox), X) * 2 + lax.rem(g % 2 + oc, 2)

    def peer_tp(dt):
        return lax.rem(t + dt, T)

    first = [
        pltpu.make_async_copy(visin.at[0], visl, loc.at[0]),
        pltpu.make_async_copy(slots.at[0], slotl, loc.at[1]),
        pltpu.make_async_copy(docin, docs, loc.at[2]),
    ]
    loads = [
        pltpu.make_async_copy(hid.at[:, mine], hown.at[pl.ds(V, tok)], loc.at[3]),
        pltpu.make_async_copy(wk, w.at[:, pl.ds(0, kvc)], loc.at[4]),
        pltpu.make_async_copy(wv, w.at[:, pl.ds(kvc, kvc)], loc.at[5]),
    ]
    qloads = [
        pltpu.make_async_copy(
            qry.at[:, pl.ds((k * QPK + h) * HEAD, HEAD)],
            qs.at[k, pl.ds(h * tok, tok)],
            loc.at[6 + k * QPK + h],
        )
        for k in range(nkv)
        for h in range(QPK)
    ]

    barrier = pltpu.get_barrier_semaphore()
    for o in offs:
        pl.semaphore_signal(barrier, inc=1, device_id={"grp": to_grp(o, 1)}, device_id_type=MESH)
    for d in range(1, S):
        pl.semaphore_signal(
            barrier, inc=1, device_id={"seq": lax.rem(s + d, S)}, device_id_type=MESH
        )
    for d in range(1, T):
        pl.semaphore_signal(barrier, inc=1, device_id={"tp": peer_tp(d)}, device_id_type=MESH)
    for c in first + loads:
        c.start()

    for c in first:
        c.wait()
    vis[...] = jnp.concatenate(
        [visl[d].astype(F32) for d in range(S)], axis=0
    ).astype(BF16)
    spread = jnp.concatenate(
        [jnp.broadcast_to(slotl[d:d + 1, :].astype(F32), (cap, cap)) for d in range(S)], axis=0
    )
    r = lax.broadcasted_iota(jnp.int32, (V, cap), 0)
    c = lax.broadcasted_iota(jnp.int32, (V, cap), 1)
    column = jnp.sum(jnp.where(r % cap == c, spread, F32(0.0)), axis=1, keepdims=True)
    column = jnp.broadcast_to(column, (V, tok)).astype(jnp.int32)
    target = lax.broadcasted_iota(jnp.int32, (V, tok), 0) // cap
    pos[...] = jnp.where(column >= 0, column + target * tok, -1)
    pl.semaphore_wait(barrier, (G - 1) + (S - 1) + (T - 1))

    def send(i, src, dst, sem):
        return pltpu.make_async_remote_copy(
            src_ref=src, dst_ref=dst, send_sem=hs.at[i, sem], recv_sem=hr.at[i, sem],
            device_id={"grp": to_grp(offs[i], 1)}, device_id_type=MESH,
        )

    def piece(i, ch):
        whom = to_grp(offs[i], 1)
        start, wide = (t * C, C) if i in far else (0, dw)
        src = pl.ds(pl.multiple_of(whom * dw + start, 128), wide)
        dst = pl.ds(pl.multiple_of(start, 128), wide) if i in far else pl.ds(0, dw)
        lo, n = (ch * q, q) if i in far else (0, tok)
        made = [send(i, hid.at[pl.ds(lo, n), src], hb.at[i, pl.ds(V + lo, n), dst], ch)]
        if ch == 0:
            made.append(send(i, vis.at[:, src], hb.at[i, pl.ds(0, V), dst], Q))
        return made

    pieces = {(i, ch): piece(i, ch) for i in far for ch in range(Q)}
    pieces |= {(i, 0): piece(i, 0) for i in near}

    def launch(ch):
        for i in far:
            for c in pieces[i, ch]:
                c.start()

    launch(0)
    if Q > 1:
        launch(1)
    for i in near:
        for c in pieces[i, 0]:
            c.start()

    vrow = pl.ds(pl.multiple_of(s * V, V), V)
    posb[vrow, :] = pos[...]
    docb[s] = docs[...]
    metas = []
    for d in range(1, S):
        whom = lax.rem(s + d, S)
        for at, (src, dst) in enumerate(((pos, posb.at[vrow]), (docs, docb.at[s]))):
            metas.append(
                pltpu.make_async_remote_copy(
                    src_ref=src, dst_ref=dst, send_sem=ms.at[d, at], recv_sem=mr.at[d, at],
                    device_id={"seq": whom}, device_id_type=MESH,
                )
            )
    for c in metas:
        c.start()
    for c in qloads:
        c.start()

    hown[0:V, :] = vis[:, mine]
    for c in loads:
        c.wait()
    total[...] = jnp.dot(hown[...], w[...], preferred_element_type=F32)

    def relay(i, ch):
        lo, n = chunks[ch]
        at = hb.at[i, pl.ds(lo, n), pl.ds(pl.multiple_of(t * C, 128), C)]
        return [
            pltpu.make_async_remote_copy(
                src_ref=at, dst_ref=at,
                send_sem=rs.at[i, ch, d], recv_sem=rr.at[i, ch, d],
                device_id={"tp": peer_tp(d)}, device_id_type=MESH,
            )
            for d in range(1, T)
        ]

    relays = {(i, ch): relay(i, ch) for i in far for ch in range(Q)}

    def giveback(i, ch):
        lo, n = chunks[ch] if i in far else (0, rows)
        return pltpu.make_async_remote_copy(
            src_ref=part.at[i, pl.ds(lo, n)], dst_ref=back.at[i, pl.ds(lo, n)],
            send_sem=bs.at[i, ch], recv_sem=br.at[i, ch],
            device_id={"grp": to_grp(offs[i], -1)}, device_id_type=MESH,
        )

    gives = {(i, ch): giveback(i, ch) for i in far for ch in range(Q)}
    gives |= {(i, 0): giveback(i, 0) for i in near}

    def finish(ch):
        lo, n = chunks[ch]
        for i in far:
            for c in relays[i, ch]:
                c.wait_recv()
        block = jnp.concatenate([hb[i, lo:lo + n, :] for i in far], axis=0)
        done = jnp.dot(block, w[...], preferred_element_type=F32).astype(BF16)
        for at, i in enumerate(far):
            part[i, lo:lo + n, :] = done[at * n:(at + 1) * n]
            gives[i, ch].start()

    def text(d, ch):
        here = kvt.at[s, pl.ds(ch * q, q)]
        return pltpu.make_async_remote_copy(
            src_ref=here, dst_ref=here,
            send_sem=ts.at[d, ch], recv_sem=tr.at[s, ch],
            device_id={"seq": d}, device_id_type=MESH,
        )

    def visual(d):
        return pltpu.make_async_remote_copy(
            src_ref=kvv.at[vrow], dst_ref=kvv.at[vrow],
            send_sem=vs.at[d], recv_sem=vr.at[d],
            device_id={"seq": lax.rem(s + d, S)}, device_id_type=MESH,
        )

    visuals = [visual(d) for d in range(1, S)]

    def settle(ch):
        lo, n = chunks[ch]
        both = total[lo:lo + n, :]
        for i in range(len(offs)):
            if (i, ch) in gives:
                gives[i, ch].wait_recv()
            both = both + back[i, lo:lo + n, :].astype(F32)
        both = both.astype(BF16)
        kvt[s, ch * q:(ch + 1) * q, :] = both[n - q:]
        if ch == 0:
            kvv[vrow, :] = both[:V]
        for d in range(S - 1, 0, -1):
            @pl.when(d > s)
            def _():
                text(d, ch).start()
        if ch == 0:
            for c in visuals:
                c.start()

    for i in near:
        for c in pieces[i, 0]:
            c.wait_recv()
        part[i] = jnp.dot(hb[i], w[...], preferred_element_type=F32).astype(BF16)
        gives[i, 0].start()
    for ch in range(Q):
        for i in far:
            for c in pieces[i, ch]:
                c.wait_recv()
            for c in relays[i, ch]:
                c.start()
        if ch + 2 < Q:
            launch(ch + 2)
        if ch >= 1:
            finish(ch - 1)
        if ch >= 2:
            settle(ch - 2)
    finish(Q - 1)
    for ch in range(max(Q - 2, 0), Q):
        settle(ch)

    for c in qloads:
        c.wait()
    for c in metas:
        c.wait_recv()
    for c in visuals:
        c.wait_recv()
    scale = 1.0 / (HEAD ** 0.5)
    lanes = lax.broadcasted_iota(jnp.int32, (S * V, tok), 1)
    krow = lax.broadcasted_iota(jnp.int32, (tok, tok), 0)
    qcol = lax.broadcasted_iota(jnp.int32, (tok, tok), 1)
    qdoc = jnp.broadcast_to(docs[...].astype(F32), (tok, tok))
    top[...] = jnp.full(top.shape, -1e30, F32)
    den[...] = jnp.zeros(den.shape, F32)
    acc[...] = jnp.zeros(acc.shape, F32)
    firsts = (((0,), (0,)), ((), ()))

    def block(j):
        pick = (posb[...] == lanes + j * tok).astype(F32).astype(BF16)
        moved = lax.dot_general(pick, kvv[...], firsts, preferred_element_type=F32)
        used = lax.dot_general(
            pick, jnp.ones((S * V, 2 * kvc), BF16), firsts, preferred_element_type=F32
        )
        kv = jnp.where(used > 0.5, moved, kvt[j].astype(F32)).astype(BF16)
        kdoc = jnp.broadcast_to(docb[j].astype(F32), (tok, tok)).T
        allowed = (krow + j * tok <= qcol + s * tok) & (kdoc == qdoc)
        bias = jnp.where(allowed, F32(0.0), F32(-1e30))
        bias = jnp.concatenate([bias] * QPK, axis=1)
        for k in range(nkv):
            key = kv[:, k * HEAD:(k + 1) * HEAD]
            value = kv[:, kvc + k * HEAD:kvc + (k + 1) * HEAD]
            scores = lax.dot_general(
                key, qs[k], (((1,), (1,)), ((), ())), preferred_element_type=F32
            ) * scale + bias
            old = top[k]
            new = jnp.maximum(old, jnp.max(scores, axis=0, keepdims=True))
            weights = jnp.exp(scores - new)
            shrink = jnp.exp(old - new)
            top[k] = new
            den[k] = den[k] * shrink + jnp.sum(weights, axis=0, keepdims=True)
            acc[k] = acc[k] * shrink + lax.dot_general(
                value, weights.astype(BF16), firsts, preferred_element_type=F32
            )

    block(s)

    def step(i, carry):
        j = s - i
        for ch in range(Q):
            there = kvt.at[j, pl.ds(ch * q, q)]
            pltpu.make_async_remote_copy(
                src_ref=there, dst_ref=there,
                send_sem=ts.at[0, ch], recv_sem=tr.at[j, ch],
                device_id={"seq": j}, device_id_type=MESH,
            ).wait_recv()
        block(j)
        return carry

    lax.fori_loop(1, s + 1, step, 0)
    for k in range(nkv):
        done = acc[k] / den[k]
        for h in range(QPK):
            at = (k * QPK + h) * HEAD
            out[:, at:at + HEAD] = done[:, h * tok:(h + 1) * tok].T.astype(out.dtype)

    for it in pieces.values():
        for c in it:
            c.wait_send()
    for it in relays.values():
        for c in it:
            c.wait_send()
    for c in gives.values():
        c.wait_send()
    for c in metas + visuals:
        c.wait_send()
    for ch in range(Q):
        for d in range(1, S):
            @pl.when(d > s)
            def _():
                text(d, ch).wait_send()


def shards(G, S, T, hidden, queries, vis_rows, vis_slot, doc_ids, w_key, w_value):
    tok, D = hidden.shape
    cap = vis_rows.shape[2]
    V = S * cap
    dw, kvc = w_key.shape
    nkv = kvc // HEAD
    Q = 4 if tok % 64 == 0 else 1
    rows = tok + V
    dma = pltpu.SemaphoreType.DMA
    hbm = pl.BlockSpec(memory_space=pltpu.HBM)
    vmem = pl.BlockSpec(memory_space=pltpu.VMEM)
    return pl.pallas_call(
        functools.partial(kernel, G, S, T, Q),
        out_shape=jax.ShapeDtypeStruct((tok, queries.shape[1]), BF16),
        in_specs=[hbm] * 7,
        out_specs=vmem,
        scratch_shapes=[
            pltpu.VMEM((dw, 2 * kvc), BF16),
            pltpu.VMEM((rows, dw), BF16),
            pltpu.VMEM((G - 1, rows, dw), BF16),
            pltpu.VMEM((G - 1, rows, 2 * kvc), BF16),
            pltpu.VMEM((G - 1, rows, 2 * kvc), BF16),
            pltpu.VMEM((rows, 2 * kvc), F32),
            pltpu.VMEM((S, tok, 2 * kvc), BF16),
            pltpu.VMEM((S * V, 2 * kvc), BF16),
            pltpu.VMEM((S * V, tok), jnp.int32),
            pltpu.VMEM((S, 1, tok), jnp.int32),
            pltpu.VMEM((nkv, QPK * tok, HEAD), BF16),
            pltpu.VMEM((nkv, 1, QPK * tok), F32),
            pltpu.VMEM((nkv, 1, QPK * tok), F32),
            pltpu.VMEM((nkv, HEAD, QPK * tok), F32),
            pltpu.VMEM((S, cap, D), BF16),
            pltpu.VMEM((V, D), BF16),
            pltpu.VMEM((S, cap), jnp.int32),
            pltpu.VMEM((V, tok), jnp.int32),
            pltpu.VMEM((1, tok), jnp.int32),
            dma((6 + nkv * QPK,)),
            dma((G - 1, Q + 1)), dma((G - 1, Q + 1)),
            dma((G - 1, Q, T)), dma((G - 1, Q, T)),
            dma((G - 1, Q)), dma((G - 1, Q)),
            dma((S, Q)), dma((S, Q)),
            dma((S,)), dma((S,)),
            dma((S, 2)), dma((S, 2)),
        ],
        compiler_params=pltpu.CompilerParams(
            collective_id=0, has_side_effects=True, vmem_limit_bytes=64 * 1024 * 1024
        ),
    )(hidden, vis_rows, queries, w_key, w_value, vis_slot, doc_ids)


def solution(mesh):
    sizes = mesh.shape
    return jax.shard_map(
        functools.partial(shards, sizes["grp"], sizes["seq"], sizes["tp"]),
        mesh=mesh,
        in_specs=(
            P(("grp", "seq"), None),
            P(("grp", "seq"), "tp"),
            P(("grp", "seq"), None, None, None),
            P(("grp", "seq"), None, None),
            P("grp", "seq"),
            P("grp", "tp"),
            P("grp", "tp"),
        ),
        out_specs=P(("grp", "seq"), "tp"),
        check_vma=False,
    )
```

time: 49.2 us -> 40.2 us (0.82)
  local copies, waits for them, and re-layouts: 8.54 us -> 1.88 us
  Pallas kernels: 40.3 us -> 37.6 us
    unnamed x11 -> x1, local copies, waits for them, and re-layouts: 6.53 us -> 1.88 us
    pallas_call x1, Pallas kernels: 40.3 us -> 37.6 us  [shards(): pl.pallas_call(functools.partial(kernel, G, S, T, Q), out_shape=jax.Shape...]
    reshape x2 -> x0, local copies, waits for them, and re-layouts: 1.78 us -> none  [the longest x1 1.02 us: shards(): vis = vis_rows.reshape(-1, D)]
where the time goes in v2:
time: 40.2 us; the launch traced here: 39.5 us
  Pallas kernels  37.6 us (94%)
  local copies, waits for them, and re-layouts  1.88 us (5%)
    pallas_call x1, Pallas kernels, shards(): pl.pallas_call(functools.partial(kernel, G, S, T, Q), out_shape=jax.Shape...  37.6 us
    unnamed x1, local copies, waits for them, and re-layouts  1.88 us

profile of v2, /device:TPU:17, one launch (start us, length us, event | category | flops | bytes accessed | tf_op | source)
XLA Modules:
  0.0 39.5 jit_solution(2544386496584117887)
XLA Ops:
  0.0 37.6 %shard_map.73 = bf16[128,2048]{1,0:T(8,128)(2,1)} custom-call(bf16[128,8192]{1,0:T(8,128)(2,1)} %hid.1, bf16[1,4,4,8192]{3,2,1,0:T(4,128)(2,1)} %visin.1, bf16[128,2048]{1,0:T(8,128)(2,1)} %qry.1, bf16[2048,256]{1,0:T(8,128)(2,1)} %wk.1, bf16[2048,256]{1,0:T(8,128)(2,1)} %wv.1, s32[1,4,4]{2,1,0:T(4,128)} %slots.1, s32[1,128]{1,0:T(1,128)} %docin.1), custom_call_target="tpu_custom_call" | custom-call | tf_op jit(solution)/shard_map/pallas_call | solution.py:334
  37.6 1.9 %copy.9 = bf16[128,2048]{1,0:T(8,128)(2,1)} copy(bf16[128,2048]{1,0:T(8,128)(2,1)} %shard_map.73) | data formatting | bytes 1048576

commit v3 on v2

--- a/solution.py
+++ b/solution.py
@@ -119,10 +119,6 @@
     launch(0)
     if Q > 1:
         launch(1)
-    for i in near:
-        for c in pieces[i, 0]:
-            c.start()
-
     vrow = pl.ds(pl.multiple_of(s * V, V), V)
     posb[vrow, :] = pos[...]
     docb[s] = docs[...]
@@ -210,7 +206,7 @@
         kvt[s, ch * q:(ch + 1) * q, :] = both[n - q:]
         if ch == 0:
             kvv[vrow, :] = both[:V]
-        for d in range(S - 1, 0, -1):
+        for d in range(1, S):
             @pl.when(d > s)
             def _():
                 text(d, ch).start()
@@ -218,6 +214,9 @@
             for c in visuals:
                 c.start()
 
+    for i in near:
+        for c in pieces[i, 0]:
+            c.start()
     for i in near:
         for c in pieces[i, 0]:
             c.wait_recv()
@@ -229,10 +228,10 @@
                 c.wait_recv()
             for c in relays[i, ch]:
                 c.start()
+        if ch >= 1:
+            finish(ch - 1)
         if ch + 2 < Q:
             launch(ch + 2)
-        if ch >= 1:
-            finish(ch - 1)
         if ch >= 2:
             settle(ch - 2)
     finish(Q - 1)

time: 40.2 us -> 39.4 us (0.980)
  the two profiles are of different devices: /device:TPU:17 before, /device:TPU:25 now
where the time goes in v3:
time: 39.4 us; the launch traced here: 39.2 us
  Pallas kernels  37.3 us (95%)
  local copies, waits for them, and re-layouts  1.88 us (5%)
    pallas_call x1, Pallas kernels, shards(): pl.pallas_call(functools.partial(kernel, G, S, T, Q), out_shape=jax.Shape...  37.3 us
    unnamed x1, local copies, waits for them, and re-layouts  1.88 us

profile of v3, /device:TPU:25, one launch (start us, length us, event | category | flops | bytes accessed | tf_op | source)
XLA Modules:
  0.0 39.2 jit_solution(10032455622096844003)
XLA Ops:
  0.0 37.3 %shard_map.73 = bf16[128,2048]{1,0:T(8,128)(2,1)} custom-call(bf16[128,8192]{1,0:T(8,128)(2,1)} %hid.1, bf16[1,4,4,8192]{3,2,1,0:T(4,128)(2,1)} %visin.1, bf16[128,2048]{1,0:T(8,128)(2,1)} %qry.1, bf16[2048,256]{1,0:T(8,128)(2,1)} %wk.1, bf16[2048,256]{1,0:T(8,128)(2,1)} %wv.1, s32[1,4,4]{2,1,0:T(4,128)} %slots.1, s32[1,128]{1,0:T(1,128)} %docin.1), custom_call_target="tpu_custom_call" | custom-call | tf_op jit(solution)/shard_map/pallas_call | solution.py:333
  37.3 1.9 %copy.9 = bf16[128,2048]{1,0:T(8,128)(2,1)} copy(bf16[128,2048]{1,0:T(8,128)(2,1)} %shard_map.73) | data formatting | bytes 1048576
